TPU v7x, 256 devices: a whole 4x4x8 slice. The times are simulated.
256 devices in a mesh: slab: 32 (over x, z), col: 4 (over y), pb: 2 (over core).
Axes of the slice: x: 4, y: 4, z: 8, core: 2. Of those that a mesh axis runs over, the one named last changes fastest.
Arguments:
- queries_raw: float32 [1024, 768], P(('slab', 'col', 'pb')), may hold values from -1.5 to 1.5
- projection: float32 [768, 768], replicated, may hold values from -0.21875 to 0.21875
- passages: bfloat16 [524288, 768], P(('slab', 'col')), may hold values from -17 to 17
- positives: int32 [1024, 4], P(('slab', 'col', 'pb')), may hold values from 0 to 524287
Outputs:
- loss: float32 [1024], P(('slab', 'col', 'pb'))
- grad_raw: float32 [1024, 768], P(('slab', 'col', 'pb'))
- grad_projection: float32 [768, 768], replicated
All inputs are finite; a program needn't handle non-finite values.
Results may differ from a plain program's by a relative error of at most 0.0053.
Values may be sent and summed in bfloat16 or wider, within the bound.
No kernel may reach another device: no remote copies, remote signals or barrier semaphores. Data moves between devices by JAX's collectives and lax.ppermute only.
A program may use at most 128 MiB of HBM per device.

v0:
```python
import jax
import jax.numpy as jnp
from jax import lax
from jax.sharding import Mesh, PartitionSpec as P

POS = 4
ALL = ("x", "z", "y", "c")
XY = ("x", "y")


def exchange(v, axes):
    return lax.all_to_all(v, axes, 0, 0, tiled=False)


def spread(v, axes):
    n = lax.axis_size(axes)
    return exchange(jnp.broadcast_to(v[None], (n,) + v.shape), axes)


def total(v):
    v = jnp.sum(spread(v, XY), axis=0)
    return jnp.sum(spread(v, "z"), axis=0)


def shards(queries_raw, projection, passages, positives):
    hp = lax.Precision.HIGHEST
    rows, dim = passages.shape
    own = queries_raw.shape[0]
    nz, nxy = (lax.axis_size("z"), lax.axis_size(XY))
    plane = nz * own
    queries = nxy * plane
    scale = 1.0 / (4.0 * rows * nz * nxy)
    bf16 = jnp.bfloat16
    raw_all = lax.all_gather(queries_raw.astype(bf16), ALL, axis=0, tiled=True)
    projected = jnp.dot(queries_raw, projection, precision=hp, preferred_element_type=jnp.float32)
    ids = jnp.concatenate([positives >> 14, positives >> 7 & 127, positives & 127], axis=1)
    ids = jnp.pad(ids, ((0, 0), (0, 128 - 3 * POS)))
    packet = jnp.concatenate([projected.astype(bf16), ids.astype(bf16)], axis=1)
    packet = spread(packet, "z").reshape(plane, dim + 128)
    packet = spread(packet, XY).reshape(queries, dim + 128)
    all_emb = packet[:, :dim]
    ids = packet[:, dim : dim + 3 * POS].astype(jnp.float32).astype(jnp.int32)
    all_pos = (ids[:, :POS] << 14) + (ids[:, POS : 2 * POS] << 7) + ids[:, 2 * POS :]
    shard = (lax.axis_index("x") * nz + lax.axis_index("z")) * lax.axis_size("y") + lax.axis_index(
        "y"
    )
    local_pos = all_pos - shard * rows
    scores = lax.dot_general(
        all_emb, passages, (((1,), (1,)), ((), ())), preferred_element_type=jnp.float32
    )
    columns = jnp.arange(rows, dtype=jnp.int32)[None, :]
    owned = [local_pos[:, slot : slot + 1] == columns for slot in range(POS)]
    partial_pos = jnp.stack(
        [jnp.sum(jnp.where(owned[slot], scores, 0.0), axis=1) for slot in range(POS)], axis=0
    )
    pos_scores = total(partial_pos).T
    loss_part = jnp.zeros((queries,), jnp.float32)
    slope_sum = jnp.zeros_like(scores)
    parts = []
    for slot in range(POS):
        sig = jax.nn.sigmoid(scores - pos_scores[:, slot : slot + 1])
        loss_part = loss_part + jnp.sum(sig, axis=1)
        slope = sig * (1.0 - sig)
        slope_sum = slope_sum + slope
        parts.append(-jnp.sum(slope, axis=1))
    sums = total(jnp.stack(parts + [loss_part], axis=0) * scale)
    pos_grad = sums[:POS].T
    grad = slope_sum * scale
    for slot in range(POS):
        grad = grad + jnp.where(owned[slot], pos_grad[:, slot : slot + 1], 0.0)
    part = jnp.dot(grad.astype(bf16), passages, preferred_element_type=jnp.float32)
    part = exchange(part.astype(bf16).reshape(nxy, plane, dim), XY)
    part = jnp.sum(part.astype(jnp.float32), axis=0).astype(bf16)
    summed = jnp.sum(spread(part, "z").astype(jnp.float32), axis=0)
    home = lax.axis_index("z") * own
    query_grad = lax.dynamic_slice_in_dim(summed, home, own, 0)
    grad_raw = jnp.dot(query_grad, projection.T, precision=hp, preferred_element_type=jnp.float32)
    first = lax.axis_index(XY) * plane + home
    loss = lax.dynamic_slice_in_dim(sums[POS], first, own, 0)
    mine = spread(summed.astype(bf16), XY).reshape(queries, dim)
    other = lax.ppermute(mine, "c", [(0, 1), (1, 0)])
    even = lax.axis_index("c") == 0
    grads = jnp.concatenate([jnp.where(even, mine, other), jnp.where(even, other, mine)], axis=0)
    sizes = [lax.axis_size(a) for a in ALL]
    raw = raw_all.reshape(*sizes, own, dim).transpose(3, 0, 2, 1, 4, 5).reshape(2 * queries, dim)
    grad_projection = lax.dot_general(
        raw, grads, (((0,), (0,)), ((), ())), preferred_element_type=jnp.float32
    )
    return (loss, grad_raw, grad_projection)


def solution(mesh):
    axes = Mesh(mesh.devices.reshape(4, 8, 4, 2), ALL)
    in_specs = (P(ALL, None), P(), P(("x", "z", "y"), None), P(ALL, None))
    out_specs = (P(ALL), P(ALL, None), P())
    return jax.shard_map(shards, mesh=axes, in_specs=in_specs, out_specs=out_specs, check_vma=False)
```

profile of v0, /device:TPU:1, one launch (start us, length us, event | category | flops | bytes accessed | tf_op | source)
XLA Modules:
  0.0 247.1 jit_solution(9730011516197225526)
XLA Ops:
  7.2 0.0 copy-start
  7.2 0.8 shift-right-arithmetic_convert_fusion
  8.0 0.8 copy-done
  8.9 1.9 convolution_convert_fusion
  10.8 0.1 fusion.19
  10.9 16.1 %all_to_all.45 = bf16[8,4,896]{2,1,0:T(4,128)(2,1)S(1)} all-to-all(bf16[8,4,896]{2,1,0:T(4,128)(2,1)S(1)} %broadcast_in_dim.93), channel_id=1, replica_groups=mesh['x'=4,'z'=8,'y'=4,'c'=2] {'z'}, dimensions={0} | all-to-all | bytes 114688 | tf_op jit(solution)/shard_map/all_to_all | solution.py:12
  27.0 1.0 broadcast_in_dim.95
  28.0 6.8 %all-to-all-start.1 = ((bf16[16,32,896]{2,1,0:T(8,128)(2,1)}), bf16[16,32,896]{2,1,0:T(8,128)(2,1)S(1)}, u32[]{:S(2)}, u32[]{:S(2)}) async-start(bf16[16,32,896]{2,1,0:T(8,128)(2,1)} %broadcast_in_dim.95), calls=%async_computation.1 | async-start | bytes 1835008 | tf_op jit(solution)/shard_map/all_to_all | solution.py:12
  34.7 13.4 %all-to-all-done.1 = bf16[16,32,896]{2,1,0:T(8,128)(2,1)S(1)} async-done(((bf16[16,32,896]{2,1,0:T(8,128)(2,1)}), bf16[16,32,896]{2,1,0:T(8,128)(2,1)S(1)}, u32[]{:S(2)}, u32[]{:S(2)}) %all-to-all-start.1) | async-done | bytes 917536 | tf_op jit(solution)/shard_map/all_to_all | solution.py:12
  48.1 0.2 fusion.11
  48.3 0.6 slice_reduce_fusion.3
  48.9 11.5 %select_reduce_fusion.3 = (f32[512]{0:T(512)S(1)}, f32[512]{0:T(512)S(1)}, f32[512]{0:T(512)S(1)}, f32[512]{0:T(512)S(1)}, f32[512,4096]{1,0:T(8,128)}) fusion(s32[512]{0:T(512)S(1)} %get-tuple-element.33, s32[512]{0:T(512)S(1)} %get-tuple-element.34, s32[512]{0:T(512)S(1)} %get-tuple-element.35, s32[512]{0:T(512)S(1)} %get-tuple-element.36, ...), kind=kOutput, calls=%fused_computation.15 | convolution fusion | flops 3246389248 | bytes 15482880 | tf_op jit(solution)/shard_map/dot_general | solution.py:48
  60.4 11.2 %all_to_all.46 = f32[16,4,512]{2,1,0:T(4,128)S(1)} all-to-all(f32[16,4,512]{2,1,0:T(4,128)S(1)} %broadcast_in_dim.97), channel_id=1, replica_groups=mesh['x'=4,'z'=8,'y'=4,'c'=2] {'x','y'}, dimensions={0} | all-to-all | bytes 262144 | tf_op jit(solution)/shard_map/all_to_all | solution.py:12
  71.6 9.6 %all_to_all.47 = f32[8,4,512]{2,1,0:T(4,128)S(1)} all-to-all(f32[8,4,512]{2,1,0:T(4,128)S(1)} %broadcast_in_dim.98), channel_id=1, replica_groups=mesh['x'=4,'z'=8,'y'=4,'c'=2] {'z'}, dimensions={0} | all-to-all | bytes 131072 | tf_op jit(solution)/shard_map/all_to_all | solution.py:12
  81.3 0.0 copy-start.1
  81.3 17.0 %fusion.28 = (f32[512]{0:T(512)S(1)}, f32[512]{0:T(512)S(1)}, f32[512,4096]{1,0:T(8,128)}, f32[512]{0:T(512)S(1)}, f32[512]{0:T(512)S(1)}, /*index=5*/f32[512,40...) fusion(f32[512,4096]{1,0:T(8,128)} %get-tuple-element.63, ...), kind=kLoop, calls=%fused_computation.70 | loop fusion | flops 67104768 | bytes 41967616 | tf_op jit(solution)/shard_map/reduce_sum | solution.py:62
  98.5 10.7 %all_to_all.48 = f32[16,5,512]{2,1,0:T(8,128)S(1)} all-to-all(f32[16,5,512]{2,1,0:T(8,128)S(1)} %broadcast_in_dim.99), channel_id=1, replica_groups=mesh['x'=4,'z'=8,'y'=4,'c'=2] {'x','y'}, dimensions={0} | all-to-all | bytes 327680 | tf_op jit(solution)/shard_map/all_to_all | solution.py:12
  109.2 0.7 broadcast_in_dim.100
  109.9 3.4 %all-to-all-start.5 = ((f32[8,5,512]{2,1,0:T(8,128)}), f32[8,5,512]{2,1,0:T(8,128)S(1)}, u32[]{:S(2)}, u32[]{:S(2)}) async-start(f32[8,5,512]{2,1,0:T(8,128)} %broadcast_in_dim.100), calls=%async_computation.5 | async-start | bytes 262144 | tf_op jit(solution)/shard_map/all_to_all | solution.py:12
  113.2 0.2 all-gather.3.cloned.1.call-start
  113.5 0.0 copy-done.1
  113.5 0.6 convert_bitcast_fusion
  114.1 0.0 all-gather.3.cloned.1.call-update
  114.1 7.0 %all-to-all-done.5 = f32[8,5,512]{2,1,0:T(8,128)S(1)} async-done(((f32[8,5,512]{2,1,0:T(8,128)}), f32[8,5,512]{2,1,0:T(8,128)S(1)}, u32[]{:S(2)}, u32[]{:S(2)}) %all-to-all-start.5) | async-done | bytes 81952 | tf_op jit(solution)/shard_map/all_to_all | solution.py:12
  121.1 20.3 %fusion.8 = bf16[512,768]{1,0:T(8,128)(2,1)S(1)} fusion(bf16[4096,768]{1,0:T(8,128)(2,1)} %param.6, f32[512,4096]{1,0:T(8,128)} %get-tuple-element.43, f32[512,4096]{1,0:T(8,128)} %get-tuple-element.49, f32[512,4096]{1,0:T(8,128)} %get-tuple-element.46, f32[512,4096]{1,0:T(8,128)} %get-tuple-element.37, f32[512]{0:T(512)S(1)} %bitcast.58, ...), kind=kOutput, calls=%fused_computation.27 | convolution fusion | flops 3274047488 | bytes 40648704 | tf_op jit(solution)/shard_map/dot_general | solution.py:71
  141.4 13.4 %all_to_all.49 = bf16[16,32,768]{2,1,0:T(8,128)(2,1)S(1)} all-to-all(bf16[16,32,768]{2,1,0:T(8,128)(2,1)S(1)} %bitcast.46), channel_id=1, replica_groups=mesh['x'=4,'z'=8,'y'=4,'c'=2] {'x','y'}, dimensions={0} | all-to-all | bytes 1572864 | tf_op jit(solution)/shard_map/all_to_all | solution.py:12
  154.8 0.1 reduce_sum.181
  154.9 13.1 %all_to_all.50 = bf16[8,32,768]{2,1,0:T(8,128)(2,1)S(1)} all-to-all(bf16[8,32,768]{2,1,0:T(8,128)(2,1)S(1)} %broadcast_in_dim.109), channel_id=1, replica_groups=mesh['x'=4,'z'=8,'y'=4,'c'=2] {'z'}, dimensions={0} | all-to-all | bytes 786432 | tf_op jit(solution)/shard_map/all_to_all | solution.py:12
  168.0 0.1 convert_reduce_fusion
  168.1 0.1 broadcast_in_dim.110
  168.2 13.4 %all_to_all.51 = bf16[16,32,768]{2,1,0:T(8,128)(2,1)S(1)} all-to-all(bf16[16,32,768]{2,1,0:T(8,128)(2,1)S(1)} %broadcast_in_dim.110), channel_id=1, replica_groups=mesh['x'=4,'z'=8,'y'=4,'c'=2] {'x','y'}, dimensions={0} | all-to-all | bytes 1572864 | tf_op jit(solution)/shard_map/all_to_all | solution.py:12
  181.6 10.9 %collective-permute-start = (bf16[512,768]{1,0:T(8,128)(2,1)S(1)}, bf16[512,768]{1,0:T(8,128)(2,1)}, u32[]{:S(2)}, u32[]{:S(2)}) collective-permute-start(bf16[512,768]{1,0:T(8,128)(2,1)S(1)} %bitcast.42), channel_id=1, source_target_pairs={{0,1},{1,0},{2,3},{3,2},{4,5},{5,4},{6,7},{7,6},{8,9},{9,8},{10,11... | collective-permute-start | bytes 2359304 | tf_op jit(solution)/shard_map/ppermute | solution.py:81
  192.5 0.6 dynamic-slice_bitcast_fusion
  193.0 2.6 %fusion.13 = f32[4,768]{1,0:T(4,128)} fusion(f32[768,768]{1,0:T(8,128)S(1)} %copy-done, f32[32,768]{1,0:T(8,128)S(1)} %convert_reduce_fusion, s32[]{:T(128)S(6)} %select_n.53), kind=kOutput, calls=%fused_computation.44 | convolution fusion | flops 28311552 | bytes 2383876 | tf_op jit(solution)/shard_map/dot_general | solution.py:77
  195.7 28.9 %all-gather.3.cloned.1.call-done = bf16[256,4,768]{2,1,0:T(4,128)(2,1)} async-done(((bf16[1,4,768]{2,1,0:T(4,128)(2,1)}), bf16[256,4,768]{2,1,0:T(4,128)(2,1)}) %all-gather.3.cloned.1.call-update) | async-done | bytes 1572880 | tf_op jit(solution)/shard_map/all_gather | solution.py:34
  224.6 3.4 %copy.31 = bf16[4,8,4,2,4,768]{5,4,1,2,0,3:T(4,128)(2,1)} copy(bf16[4,8,4,2,4,768]{5,4,3,2,1,0:T(4,128)(2,1)} %bitcast.43) | data formatting | bytes 3145728 | tf_op jit(solution)/shard_map/reshape | solution.py:85
  228.0 3.7 %reshape.137 = bf16[1024,768]{1,0:T(8,128)(2,1)} reshape(bf16[2,4,4,8,4,768]{5,4,3,2,1,0:T(4,128)(2,1)} %bitcast.41) | data formatting | bytes 3145728 | tf_op jit(solution)/shard_map/reshape | solution.py:85
  231.7 0.0 collective-permute-done
  231.7 1.2 broadcast_select_fusion.1
  232.9 4.3 %convolution_bitcast_fusion = f32[768,768]{0,1:T(8,128)} fusion(bf16[1024,768]{1,0:T(8,128)(2,1)} %reshape.137, bf16[512,768]{1,0:T(8,128)(2,1)S(1)} %get-tuple-element.51, bf16[512,768]{1,0:T(8,128)(2,1)S(1)} %get-tuple-element.50), kind=kOutput, calls=%fused_computation.22 | convolution fusion | flops 1211105280 | bytes 5505024 | tf_op jit(solution)/shard_map/dot_general | solution.py:86
  237.2 3.0 %copy.22 = f32[768,768]{1,0:T(8,128)} copy(f32[768,768]{0,1:T(8,128)} %convolution_bitcast_fusion) | data formatting | bytes 4718592
  (25 shorter events, 0.4 us)
Async XLA Ops:
  7.2 1.7 copy-start
  28.0 20.1 %all-to-all-start.1 = ((bf16[16,32,896]{2,1,0:T(8,128)(2,1)}), bf16[16,32,896]{2,1,0:T(8,128)(2,1)S(1)}, u32[]{:S(2)}, u32[]{:S(2)}) async-start(bf16[16,32,896]{2,1,0:T(8,128)(2,1)} %broadcast_in_dim.95), calls=%async_computation.1 | async-start | bytes 1835008 | tf_op jit(solution)/shard_map/all_to_all | solution.py:12
  81.3 32.2 %copy-start.1 = (f32[4,768]{1,0:T(4,128)S(1)}, f32[4,768]{1,0:T(4,128)}, u32[]{:S(2)}) copy-start(f32[4,768]{1,0:T(4,128)} %param.4) | copy-start | bytes 36868
  109.9 11.2 %all-to-all-start.5 = ((f32[8,5,512]{2,1,0:T(8,128)}), f32[8,5,512]{2,1,0:T(8,128)S(1)}, u32[]{:S(2)}, u32[]{:S(2)}) async-start(f32[8,5,512]{2,1,0:T(8,128)} %broadcast_in_dim.100), calls=%async_computation.5 | async-start | bytes 262144 | tf_op jit(solution)/shard_map/all_to_all | solution.py:12
  113.2 111.3 %all-gather.3.cloned.1.call-start = ((), (), s32[]{:S(2)}) async-start(), calls=%async_computation.9 | async-start | bytes 1579008 | tf_op jit(solution)/shard_map/all_gather | solution.py:34
  181.6 50.1 %collective-permute-start = (bf16[512,768]{1,0:T(8,128)(2,1)S(1)}, bf16[512,768]{1,0:T(8,128)(2,1)}, u32[]{:S(2)}, u32[]{:S(2)}) collective-permute-start(bf16[512,768]{1,0:T(8,128)(2,1)S(1)} %bitcast.42), channel_id=1, source_target_pairs={{0,1},{1,0},{2,3},{3,2},{4,5},{5,4},{6,7},{7,6},{8,9},{9,8},{10,11... | collective-permute-start | bytes 2359304 | tf_op jit(solution)/shard_map/ppermute | solution.py:81
Sparse Core Ops, SparseCore 0:
  117.8 106.7 all-gather.2
where the time goes:
time: 248 us; the launch traced here: 247 us
  blocking collectives  87.4 us (35%)
  waiting for transfers between devices  49.3 us (20%)
  matrix products  40.5 us (16%)
  starting transfers between devices  21.2 us (9%)
  other arithmetic  20.4 us (8%)
  between operations  14.2 us (6%)
  local copies, waits for them, and re-layouts  14.1 us (6%)
    all_to_all x7, blocking collectives, exchange(): return lax.all_to_all(v, axes, 0, 0, tiled=False)  87.4 us
    all_gather x1, waiting for transfers between devices, shards(): raw_all = lax.all_gather(queries_raw.astype(bf16), ALL, axis=0, tiled=True)  28.9 us
    all_to_all x2, waiting for transfers between devices, exchange(): return lax.all_to_all(v, axes, 0, 0, tiled=False)  20.3 us
    dot_general x1, matrix products, shards(): jnp.dot(grad.astype(bf16), passages, preferred_element_type=jnp.float32)  20.3 us
    reduce_sum x1, other arithmetic, shards(): loss_part = loss_part + jnp.sum(sig, axis=1)  17 us
    dot_general x1, matrix products, shards(): lax.dot_general(all_emb, passages, (((1,), (1,)), ((), ())), preferred_el...  11.5 us
    ppermute x1, starting transfers between devices, shards(): other = lax.ppermute(mine, 'c', [(0, 1), (1, 0)])  10.9 us
    all_to_all x2, starting transfers between devices, exchange(): return lax.all_to_all(v, axes, 0, 0, tiled=False)  10.1 us
  transfers between devices with their start and end apart: 4, of which 3 were waited for; matrix products, arithmetic and copies ran while one was open for 13% of the time, Pallas kernels for 0%

commit v1 on v0

--- a/solution.py
+++ b/solution.py
@@ -31,7 +31,16 @@
     queries = nxy * plane
     scale = 1.0 / (4.0 * rows * nz * nxy)
     bf16 = jnp.bfloat16
-    raw_all = lax.all_gather(queries_raw.astype(bf16), ALL, axis=0, tiled=True)
+    my_tile = queries_raw.astype(bf16)
+    raw_all = jnp.concatenate(
+        jax.lax.all_to_all(
+            jnp.stack([my_tile for _ in range(jax.lax.axis_size(ALL))]),
+            split_axis=0,
+            concat_axis=0,
+            axis_name=ALL,
+        ),
+        axis=0,
+    )
     projected = jnp.dot(queries_raw, projection, precision=hp, preferred_element_type=jnp.float32)
     ids = jnp.concatenate([positives >> 14, positives >> 7 & 127, positives & 127], axis=1)
     ids = jnp.pad(ids, ((0, 0), (0, 128 - 3 * POS)))

time: 248 us -> 252 us (1.016)
  between operations: 14.2 us -> 0.86 us
  waiting for transfers between devices: 49.3 us -> 59.3 us
  starting transfers between devices: 21.2 us -> 30.1 us
  blocking collectives: 87.4 us -> 84.3 us
    all_to_all x0 -> x1, waiting for transfers between devices: none -> 35.7 us  [shards(): jax.lax.all_to_all(jnp.stack([my_tile for _ in range(jax.lax.axis_size(AL...]
    all_gather x1 -> x0, waiting for transfers between devices: 28.9 us -> none  [shards(): raw_all = lax.all_gather(queries_raw.astype(bf16), ALL, axis=0, tiled=True)]
    all_to_all x0 -> x1, starting transfers between devices: none -> 17.1 us  [shards(): jax.lax.all_to_all(jnp.stack([my_tile for _ in range(jax.lax.axis_size(AL...]
    ppermute x1, starting transfers between devices: 10.9 us -> 2.66 us  [shards(): other = lax.ppermute(mine, 'c', [(0, 1), (1, 0)])]
    transpose x0 -> x1, local copies, waits for them, and re-layouts: none -> 3.38 us  [shards(): raw_all.reshape(*sizes, own, dim).transpose(3, 0, 2, 1, 4, 5)]
    reshape x2 -> x1, local copies, waits for them, and re-layouts: 7.1 us -> 3.73 us  [shards(): raw_all.reshape(*sizes, own, dim).transpose(3, 0, 2, 1, 4, 5)]
    all_to_all x2, waiting for transfers between devices: 20.3 us -> 23.6 us  [exchange(): return lax.all_to_all(v, axes, 0, 0, tiled=False)]
    all_to_all x7, blocking collectives: 87.4 us -> 84.3 us  [exchange(): return lax.all_to_all(v, axes, 0, 0, tiled=False)]
  transfers between devices with their start and end apart: 4 -> 4, of which waited for: 3 -> 3; matrix products, arithmetic and copies ran while one was open for 13% -> 4% of each run, Pallas kernels for 0% -> 0%
where the time goes in v1:
time: 252 us; the launch traced here: 251 us
  blocking collectives  84.3 us (33%)
  waiting for transfers between devices  59.3 us (24%)
  matrix products  40.6 us (16%)
  starting transfers between devices  30.1 us (12%)
  other arithmetic  19.8 us (8%)
  local copies, waits for them, and re-layouts  15.8 us (6%)
    all_to_all x7, blocking collectives, exchange(): return lax.all_to_all(v, axes, 0, 0, tiled=False)  84.3 us
    all_to_all x1, waiting for transfers between devices, shards(): jax.lax.all_to_all(jnp.stack([my_tile for _ in range(jax.lax.axis_size(AL...  35.7 us
    all_to_all x2, waiting for transfers between devices, exchange(): return lax.all_to_all(v, axes, 0, 0, tiled=False)  23.6 us
    dot_general x1, matrix products, shards(): jnp.dot(grad.astype(bf16), passages, preferred_element_type=jnp.float32)  20.3 us
    all_to_all x1, starting transfers between devices, shards(): jax.lax.all_to_all(jnp.stack([my_tile for _ in range(jax.lax.axis_size(AL...  17.1 us
    reduce_sum x1, other arithmetic, shards(): loss_part = loss_part + jnp.sum(sig, axis=1)  17.1 us
    dot_general x1, matrix products, shards(): lax.dot_general(all_emb, passages, (((1,), (1,)), ((), ())), preferred_el...  11.5 us
    all_to_all x2, starting transfers between devices, exchange(): return lax.all_to_all(v, axes, 0, 0, tiled=False)  10.4 us
  transfers between devices with their start and end apart: 4, of which 3 were waited for; matrix products, arithmetic and copies ran while one was open for 4% of the time, Pallas kernels for 0%

profile of v1, /device:TPU:1, one launch (start us, length us, event | category | flops | bytes accessed | tf_op | source)
XLA Modules:
  0.0 250.9 jit_solution(1856981258674896422)
XLA Ops:
  0.6 0.0 copy-start
  0.6 0.8 shift-right-arithmetic_convert_fusion
  1.5 0.8 copy-done
  2.3 1.9 convolution_convert_fusion
  4.2 0.1 fusion.19
  4.4 16.1 %all_to_all.50 = bf16[8,4,896]{2,1,0:T(4,128)(2,1)S(1)} all-to-all(bf16[8,4,896]{2,1,0:T(4,128)(2,1)S(1)} %broadcast_in_dim.93), channel_id=1, replica_groups=mesh['x'=4,'z'=8,'y'=4,'c'=2] {'z'}, dimensions={0} | all-to-all | bytes 114688 | tf_op jit(solution)/shard_map/all_to_all | solution.py:12
  20.4 1.0 broadcast_in_dim.95
  21.4 6.8 %all-to-all-start.1 = ((bf16[16,32,896]{2,1,0:T(8,128)(2,1)}), bf16[16,32,896]{2,1,0:T(8,128)(2,1)S(1)}, u32[]{:S(2)}, u32[]{:S(2)}) async-start(bf16[16,32,896]{2,1,0:T(8,128)(2,1)} %broadcast_in_dim.95), calls=%async_computation.1 | async-start | bytes 1835008 | tf_op jit(solution)/shard_map/all_to_all | solution.py:12
  28.2 13.4 %all-to-all-done.1 = bf16[16,32,896]{2,1,0:T(8,128)(2,1)S(1)} async-done(((bf16[16,32,896]{2,1,0:T(8,128)(2,1)}), bf16[16,32,896]{2,1,0:T(8,128)(2,1)S(1)}, u32[]{:S(2)}, u32[]{:S(2)}) %all-to-all-start.1) | async-done | bytes 917536 | tf_op jit(solution)/shard_map/all_to_all | solution.py:12
  41.6 0.2 fusion.11
  41.8 0.6 slice_reduce_fusion.3
  42.4 11.5 %select_reduce_fusion.3 = (f32[512]{0:T(512)S(1)}, f32[512]{0:T(512)S(1)}, f32[512]{0:T(512)S(1)}, f32[512]{0:T(512)S(1)}, f32[512,4096]{1,0:T(8,128)}) fusion(s32[512]{0:T(512)S(1)} %get-tuple-element.30, s32[512]{0:T(512)S(1)} %get-tuple-element.31, s32[512]{0:T(512)S(1)} %get-tuple-element.32, s32[512]{0:T(512)S(1)} %get-tuple-element.33, ...), kind=kOutput, calls=%fused_computation.15 | convolution fusion | flops 3246389248 | bytes 15482880 | tf_op jit(solution)/shard_map/dot_general | solution.py:57
  53.9 11.2 %all_to_all.51 = f32[16,4,512]{2,1,0:T(4,128)S(1)} all-to-all(f32[16,4,512]{2,1,0:T(4,128)S(1)} %broadcast_in_dim.97), channel_id=1, replica_groups=mesh['x'=4,'z'=8,'y'=4,'c'=2] {'x','y'}, dimensions={0} | all-to-all | bytes 262144 | tf_op jit(solution)/shard_map/all_to_all | solution.py:12
  65.1 9.6 %all_to_all.52 = f32[8,4,512]{2,1,0:T(4,128)S(1)} all-to-all(f32[8,4,512]{2,1,0:T(4,128)S(1)} %broadcast_in_dim.98), channel_id=1, replica_groups=mesh['x'=4,'z'=8,'y'=4,'c'=2] {'z'}, dimensions={0} | all-to-all | bytes 131072 | tf_op jit(solution)/shard_map/all_to_all | solution.py:12
  74.8 17.1 %fusion.28 = (f32[512]{0:T(512)S(1)}, f32[512]{0:T(512)S(1)}, f32[512,4096]{1,0:T(8,128)}, f32[512]{0:T(512)S(1)}, f32[512]{0:T(512)S(1)}, /*index=5*/f32[512,40...) fusion(f32[512,4096]{1,0:T(8,128)} %get-tuple-element.60, ...), kind=kLoop, calls=%fused_computation.68 | loop fusion | flops 67104768 | bytes 41967616 | tf_op jit(solution)/shard_map/reduce_sum | solution.py:71
  92.0 10.7 %all_to_all.53 = f32[16,5,512]{2,1,0:T(8,128)S(1)} all-to-all(f32[16,5,512]{2,1,0:T(8,128)S(1)} %broadcast_in_dim.99), channel_id=1, replica_groups=mesh['x'=4,'z'=8,'y'=4,'c'=2] {'x','y'}, dimensions={0} | all-to-all | bytes 327680 | tf_op jit(solution)/shard_map/all_to_all | solution.py:12
  102.7 10.3 %all_to_all.54 = f32[8,5,512]{2,1,0:T(8,128)S(1)} all-to-all(f32[8,5,512]{2,1,0:T(8,128)S(1)} %broadcast_in_dim.100), channel_id=1, replica_groups=mesh['x'=4,'z'=8,'y'=4,'c'=2] {'z'}, dimensions={0} | all-to-all | bytes 163840 | tf_op jit(solution)/shard_map/all_to_all | solution.py:12
  113.1 0.0 copy-start.1
  113.1 20.3 %fusion.8 = bf16[512,768]{1,0:T(8,128)(2,1)S(1)} fusion(bf16[4096,768]{1,0:T(8,128)(2,1)} %param.6, f32[512,4096]{1,0:T(8,128)} %get-tuple-element.40, f32[512,4096]{1,0:T(8,128)} %get-tuple-element.46, f32[512,4096]{1,0:T(8,128)} %get-tuple-element.43, f32[512,4096]{1,0:T(8,128)} %get-tuple-element.34, f32[512]{0:T(512)S(1)} %bitcast.53, ...), kind=kOutput, calls=%fused_computation.26 | convolution fusion | flops 3274047488 | bytes 40648704 | tf_op jit(solution)/shard_map/dot_general | solution.py:80
  133.4 13.4 %all_to_all.55 = bf16[16,32,768]{2,1,0:T(8,128)(2,1)S(1)} all-to-all(bf16[16,32,768]{2,1,0:T(8,128)(2,1)S(1)} %bitcast.41), channel_id=1, replica_groups=mesh['x'=4,'z'=8,'y'=4,'c'=2] {'x','y'}, dimensions={0} | all-to-all | bytes 1572864 | tf_op jit(solution)/shard_map/all_to_all | solution.py:12
  146.8 0.1 reduce_sum.181
  146.9 13.1 %all_to_all.56 = bf16[8,32,768]{2,1,0:T(8,128)(2,1)S(1)} all-to-all(bf16[8,32,768]{2,1,0:T(8,128)(2,1)S(1)} %broadcast_in_dim.109), channel_id=1, replica_groups=mesh['x'=4,'z'=8,'y'=4,'c'=2] {'z'}, dimensions={0} | all-to-all | bytes 786432 | tf_op jit(solution)/shard_map/all_to_all | solution.py:12
  160.0 0.1 convert_reduce_fusion
  160.1 1.0 broadcast_in_dim.110
  161.1 3.6 %all-to-all-start.8 = ((bf16[16,32,768]{2,1,0:T(8,128)(2,1)}), bf16[16,32,768]{2,1,0:T(8,128)(2,1)S(1)}, u32[]{:S(2)}, u32[]{:S(2)}) async-start(bf16[16,32,768]{2,1,0:T(8,128)(2,1)} %broadcast_in_dim.110), calls=%async_computation.8 | async-start | bytes 1572864 | tf_op jit(solution)/shard_map/all_to_all | solution.py:12
  164.7 0.0 copy-done.1
  164.7 10.3 %all-to-all-done.8 = bf16[16,32,768]{2,1,0:T(8,128)(2,1)S(1)} async-done(((bf16[16,32,768]{2,1,0:T(8,128)(2,1)}), bf16[16,32,768]{2,1,0:T(8,128)(2,1)S(1)}, u32[]{:S(2)}, u32[]{:S(2)}) %all-to-all-start.8) | async-done | bytes 786464 | tf_op jit(solution)/shard_map/all_to_all | solution.py:12
  175.0 1.5 stack.20
  176.6 17.1 %all-to-all-start.9 = ((bf16[256,4,768]{2,1,0:T(4,128)(2,1)}), bf16[256,4,768]{2,1,0:T(4,128)(2,1)}, u32[]{:S(2)}, u32[]{:S(2)}) async-start(bf16[256,4,768]{2,1,0:T(4,128)(2,1)} %stack.20), calls=%async_computation.9 | async-start | bytes 3145728 | tf_op jit(solution)/shard_map/all_to_all | solution.py:36
  193.7 2.7 %collective-permute-start = (bf16[512,768]{1,0:T(8,128)(2,1)S(1)}, bf16[512,768]{1,0:T(8,128)(2,1)}, u32[]{:S(2)}, u32[]{:S(2)}) collective-permute-start(bf16[512,768]{1,0:T(8,128)(2,1)S(1)} %bitcast.38), channel_id=1, source_target_pairs={{0,1},{1,0},{2,3},{3,2},{4,5},{5,4},{6,7},{7,6},{8,9},{9,8},{10,11... | collective-permute-start | bytes 2359304 | tf_op jit(solution)/shard_map/ppermute | solution.py:90
  196.3 0.6 dynamic-slice_bitcast_fusion
  196.9 2.6 %fusion.13 = f32[4,768]{1,0:T(4,128)} fusion(f32[768,768]{1,0:T(8,128)S(1)} %copy-done, f32[32,768]{1,0:T(8,128)S(1)} %convert_reduce_fusion, s32[]{:T(128)S(6)} %select_n.53), kind=kOutput, calls=%fused_computation.43 | convolution fusion | flops 28311552 | bytes 2383876 | tf_op jit(solution)/shard_map/dot_general | solution.py:86
  199.5 35.7 %all-to-all-done.9 = bf16[256,4,768]{2,1,0:T(4,128)(2,1)} async-done(((bf16[256,4,768]{2,1,0:T(4,128)(2,1)}), bf16[256,4,768]{2,1,0:T(4,128)(2,1)}, u32[]{:S(2)}, u32[]{:S(2)}) %all-to-all-start.9) | async-done | bytes 1572896 | tf_op jit(solution)/shard_map/all_to_all | solution.py:36
  235.2 3.4 %copy.18 = bf16[2,4,4,8,4,768]{5,4,3,2,1,0:T(4,128)(2,1)} copy(bf16[2,4,4,8,4,768]{5,4,0,2,3,1:T(4,128)(2,1)} %bitcast.24) | data formatting | bytes 3145728 | tf_op jit(solution)/shard_map/transpose | solution.py:94
  238.6 3.7 %reshape.135 = bf16[1024,768]{1,0:T(8,128)(2,1)} reshape(bf16[2,4,4,8,4,768]{5,4,3,2,1,0:T(4,128)(2,1)} %copy.18) | data formatting | bytes 3145728 | tf_op jit(solution)/shard_map/reshape | solution.py:94
  242.3 0.0 collective-permute-done
  242.3 1.2 broadcast_select_fusion.1
  243.5 4.3 %convolution_bitcast_fusion = f32[768,768]{0,1:T(8,128)} fusion(bf16[1024,768]{1,0:T(8,128)(2,1)} %reshape.135, bf16[512,768]{1,0:T(8,128)(2,1)S(1)} %get-tuple-element.48, bf16[512,768]{1,0:T(8,128)(2,1)S(1)} %get-tuple-element.47), kind=kOutput, calls=%fused_computation.22 | convolution fusion | flops 1211105280 | bytes 5505024 | tf_op jit(solution)/shard_map/dot_general | solution.py:95
  247.8 3.0 %copy.19 = f32[768,768]{1,0:T(8,128)} copy(f32[768,768]{0,1:T(8,128)} %convolution_bitcast_fusion) | data formatting | bytes 4718592
  (27 shorter events, 0.4 us)
Async XLA Ops:
  0.6 1.7 copy-start
  21.4 20.1 %all-to-all-start.1 = ((bf16[16,32,896]{2,1,0:T(8,128)(2,1)}), bf16[16,32,896]{2,1,0:T(8,128)(2,1)S(1)}, u32[]{:S(2)}, u32[]{:S(2)}) async-start(bf16[16,32,896]{2,1,0:T(8,128)(2,1)} %broadcast_in_dim.95), calls=%async_computation.1 | async-start | bytes 1835008 | tf_op jit(solution)/shard_map/all_to_all | solution.py:12
  113.1 51.6 %copy-start.1 = (f32[4,768]{1,0:T(4,128)S(1)}, f32[4,768]{1,0:T(4,128)}, u32[]{:S(2)}) copy-start(f32[4,768]{1,0:T(4,128)} %param.4) | copy-start | bytes 36868
  161.1 13.9 %all-to-all-start.8 = ((bf16[16,32,768]{2,1,0:T(8,128)(2,1)}), bf16[16,32,768]{2,1,0:T(8,128)(2,1)S(1)}, u32[]{:S(2)}, u32[]{:S(2)}) async-start(bf16[16,32,768]{2,1,0:T(8,128)(2,1)} %broadcast_in_dim.110), calls=%async_computation.8 | async-start | bytes 1572864 | tf_op jit(solution)/shard_map/all_to_all | solution.py:12
  176.6 58.6 %all-to-all-start.9 = ((bf16[256,4,768]{2,1,0:T(4,128)(2,1)}), bf16[256,4,768]{2,1,0:T(4,128)(2,1)}, u32[]{:S(2)}, u32[]{:S(2)}) async-start(bf16[256,4,768]{2,1,0:T(4,128)(2,1)} %stack.20), calls=%async_computation.9 | async-start | bytes 3145728 | tf_op jit(solution)/shard_map/all_to_all | solution.py:36
  193.7 48.6 %collective-permute-start = (bf16[512,768]{1,0:T(8,128)(2,1)S(1)}, bf16[512,768]{1,0:T(8,128)(2,1)}, u32[]{:S(2)}, u32[]{:S(2)}) collective-permute-start(bf16[512,768]{1,0:T(8,128)(2,1)S(1)} %bitcast.38), channel_id=1, source_target_pairs={{0,1},{1,0},{2,3},{3,2},{4,5},{5,4},{6,7},{7,6},{8,9},{9,8},{10,11... | collective-permute-start | bytes 2359304 | tf_op jit(solution)/shard_map/ppermute | solution.py:90
